TPU v7x, 256 devices: a whole 4x4x8 slice. The times are simulated.
256 devices in a mesh: wa: 32 (over x, z), gz: 8 (over y, core).
Axes of the slice: x: 4, y: 4, z: 8, core: 2. Of those that a mesh axis runs over, the one named last changes fastest.
Arguments:
- tensor: float32 [4, 64, 1024, 1024], P(None, 'gz', 'wa')
- start: float32 [1024, 128], replicated, may hold values from -6 to 6
Outputs:
- factor: float32 [1024, 128], replicated
- core: float32 [4, 64, 128, 1024], P(None, 'gz', None, 'wa')
All inputs are finite; a program needn't handle non-finite values.
Results may differ from a plain program's by a relative error of at most 0.00018.
Values sent between devices are 32-bit elements; how exact they have to be, the bound alone decides.
A program may use at most 128 MiB of HBM per device.

v0:
```python
import jax
import jax.numpy as jnp
from jax import lax
from jax.sharding import PartitionSpec as P

ITERS = 4


def orthonormal(image_rows, small):
    lower = jnp.linalg.cholesky(small)
    return lax.linalg.triangular_solve(
        lower, image_rows, left_side=False, lower=True, transpose_a=True
    )


def per_device(tensor, start):
    regrouped = lax.all_to_all(tensor, "wa", split_axis=3, concat_axis=2, tiled=True)
    count_total = (
        regrouped.shape[0]
        * regrouped.shape[1]
        * lax.axis_size("gz")
        * regrouped.shape[3]
        * lax.axis_size("wa")
    )
    local_gram = jnp.einsum("szay,szby->ab", regrouped, regrouped, precision=lax.Precision.HIGHEST)
    local_gram = local_gram * (1.0 / count_total)
    basis = start
    gram = lax.psum(local_gram, ("wa", "gz"))
    for step in range(ITERS):
        image = jnp.dot(gram, basis, precision=lax.Precision.HIGHEST)
        small = jnp.dot(image.T, image, precision=lax.Precision.HIGHEST)
        basis = orthonormal(image, small)
    core = jnp.einsum("ar,szay->szry", basis, regrouped, precision=lax.Precision.HIGHEST)
    return (basis, core)


def solution(mesh):
    placed = (P(None, "gz", "wa", None), P())
    return jax.shard_map(
        per_device,
        mesh=mesh,
        in_specs=placed,
        out_specs=(P(), P(None, "gz", None, "wa")),
        check_vma=False,
    )
```

profile of v0, /device:TPU:1, one launch (start us, length us, event | category | flops | bytes accessed | tf_op | source)
XLA Modules:
  0.0 618.0 jit_solution(2813695630166431279)
XLA Ops:
  7.2 14.4 %copy.11 = f32[4,8,32,1024]{2,1,0,3:T(8,128)} copy(f32[4,8,32,1024]{3,2,1,0:T(8,128)} %param.5) | data formatting | bytes 8388608 | tf_op args[0]
  21.6 16.0 %reshape.31 = f32[32,1,32768]{2,1,0:T(1,128)} reshape(f32[1024,4,8,32]{3,2,1,0:T(8,128)} %bitcast.86) | data formatting | bytes 8388608
  37.6 104.0 %all_to_all.18 = f32[32,1,32768]{2,1,0:T(1,128)} all-to-all(f32[32,1,32768]{2,1,0:T(1,128)} %reshape.31), channel_id=1, replica_groups=mesh['wa'=32,'gz'=8] {'wa'}, dimensions={0} | all-to-all | bytes 8388608 | tf_op jit(solution)/shard_map/all_to_all | solution.py:17
  142.1 13.7 %reduce.4 = f32[32,32768]{1,0:T(8,128)} reduce(f32[32,1,32768]{2,1,0:T(1,128)} %all_to_all.18, f32[]{:T(128)} %broadcast.39), dimensions={1}, to_apply=%all_to_all.13.reduce_sub_computation | reduce | bytes 8388612 | tf_op jit(solution)/shard_map/all_to_all | solution.py:17
  155.8 9.8 %reshape.32 = f32[1024,4,8,32]{3,2,1,0:T(8,128)} reshape(f32[32,32768]{1,0:T(8,128)} %reduce.4) | data formatting | bytes 8388608
  165.6 17.7 %copy.23 = f32[4,8,32,32,32]{2,3,4,1,0:T(8,128)} copy(f32[4,8,32,32,32]{2,1,0,4,3:T(8,128)} %bitcast.87) | data formatting | bytes 8388608 | tf_op jit(solution)/shard_map/all_to_all | solution.py:17
  183.3 13.7 %all_to_all.16 = f32[4,8,1024,32]{2,3,1,0:T(8,128)} reshape(f32[4,8,32,32,32]{3,2,4,1,0:T(8,128)} %bitcast.88) | data formatting | bytes 8388608 | tf_op jit(solution)/shard_map/all_to_all | solution.py:17
  197.0 17.8 %bitcast_multiply_fusion = f32[1024,1024]{1,0:T(8,128)} fusion(f32[4,8,1024,32]{2,3,1,0:T(8,128)} %all_to_all.16), kind=kOutput, calls=%fused_computation.1 | convolution fusion | flops 12885950464 | bytes 8388608 | tf_op jit(solution)/shard_map/szay,szby->ab/dot_general | solution.py:25
  214.8 268.0 %all-reduce.2.cloned.1.call-done = f32[1024,1024]{1,0:T(8,128)} async-done(((f32[1024,1024]{1,0:T(8,128)}), f32[1024,1024]{1,0:T(8,128)}) %all-reduce.2.cloned.1.call-update) | async-done | bytes 4194320 | tf_op jit(solution)/shard_map/psum | solution.py:28
  482.8 5.6 fusion.20
  488.5 1.0 fusion.21
  489.6 11.7 %cholesky.74 = f32[128,128]{1,0:T(8,128)S(1)} custom-call(f32[128,128]{1,0:T(8,128)S(1)} %fusion.13), custom_call_target="Cholesky" | custom-call | tf_op jit(solution)/shard_map/jit(cholesky)/cholesky | solution.py:10
  502.6 9.8 %custom-call.8 = f32[1,128,128]{1,2,0:T(8,128)S(1)} custom-call(f32[1,128,128]{2,1,0:T(8,128)S(1)} %fusion.1), custom_call_target="InvertDiagBlocksLowerTriangular" | custom-call | tf_op jit(solution)/shard_map/triangular_solve/custom-call.0 | solution.py:11
  513.1 5.4 fusion.22
  518.5 1.0 fusion.23
  519.6 11.7 %cholesky.85 = f32[128,128]{1,0:T(8,128)S(1)} custom-call(f32[128,128]{1,0:T(8,128)S(1)} %fusion.11), custom_call_target="Cholesky" | custom-call | tf_op jit(solution)/shard_map/jit(cholesky)/cholesky | solution.py:10
  532.7 9.8 %custom-call.9 = f32[1,128,128]{1,2,0:T(8,128)S(1)} custom-call(f32[1,128,128]{2,1,0:T(8,128)S(1)} %fusion.2), custom_call_target="InvertDiagBlocksLowerTriangular" | custom-call | tf_op jit(solution)/shard_map/triangular_solve/custom-call.0 | solution.py:11
  543.2 5.4 fusion.24
  549.7 11.7 %cholesky.96 = f32[128,128]{1,0:T(8,128)S(1)} custom-call(f32[128,128]{1,0:T(8,128)S(1)} %fusion.9), custom_call_target="Cholesky" | custom-call | tf_op jit(solution)/shard_map/jit(cholesky)/cholesky | solution.py:10
  562.8 9.8 %custom-call.10 = f32[1,128,128]{1,2,0:T(8,128)S(1)} custom-call(f32[1,128,128]{2,1,0:T(8,128)S(1)} %fusion.3), custom_call_target="InvertDiagBlocksLowerTriangular" | custom-call | tf_op jit(solution)/shard_map/triangular_solve/custom-call.0 | solution.py:11
  573.2 5.5 fusion.26
  579.9 11.7 %cholesky.107 = f32[128,128]{1,0:T(8,128)S(1)} custom-call(f32[128,128]{1,0:T(8,128)S(1)} %fusion.7), custom_call_target="Cholesky" | custom-call | tf_op jit(solution)/shard_map/jit(cholesky)/cholesky | solution.py:10
  592.9 9.8 %custom-call.11 = f32[1,128,128]{1,2,0:T(8,128)S(1)} custom-call(f32[1,128,128]{2,1,0:T(8,128)S(1)} %fusion.4), custom_call_target="InvertDiagBlocksLowerTriangular" | custom-call | tf_op jit(solution)/shard_map/triangular_solve/custom-call.0 | solution.py:11
  603.4 6.4 %convolution_bitcast_fusion.3 = f32[4,8,128,32]{2,3,1,0:T(8,128)} fusion(f32[4,8,1024,32]{2,3,1,0:T(8,128)} %all_to_all.16, f32[128,1024]{1,0:T(8,128)S(1)} %fusion.5), kind=kOutput, calls=%fused_computation.5 | convolution fusion | flops 1610612736 | bytes 5242880 | tf_op jit(solution)/shard_map/ar,szay->szry/dot_general | solution.py:33
  (32 shorter events, 11.9 us)
Async XLA Ops:
  7.2 475.7 %copy-start = (f32[1024,128]{1,0:T(8,128)S(1)}, f32[1024,128]{1,0:T(8,128)}, u32[]{:S(2)}) copy-start(f32[1024,128]{1,0:T(8,128)} %param.6) | copy-start | bytes 1572868
  7.2 475.7 %all-reduce.2.cloned.1.call-start = ((), (), s32[]{:S(2)}) async-start(), calls=%async_computation.1 | async-start | bytes 8388608 | tf_op jit(solution)/shard_map/psum | solution.py:28
Sparse Core Ops, SparseCore 0:
  214.9 267.8 all-reduce.1
where the time goes:
time: 627 us; the launch traced here: 618 us
  waiting for transfers between devices  268 us (43%)
  other arithmetic  105 us (17%)
  blocking collectives  104 us (17%)
  local copies, waits for them, and re-layouts  73.5 us (12%)
  matrix products  52.7 us (8%)
  between operations  14.7 us (2%)
    psum x1, waiting for transfers between devices, per_device(): gram = lax.psum(local_gram, ('wa', 'gz'))  268 us
    all_to_all x1, blocking collectives, per_device(): lax.all_to_all(tensor, 'wa', split_axis=3, concat_axis=2, tiled=True)  104 us
    another operation x12, other arithmetic, orthonormal(): lower = jnp.linalg.cholesky(small)  49.6 us
    another operation x8, other arithmetic, orthonormal(): lax.linalg.triangular_solve(lower, image_rows, left_side=False, lower=Tru...  41.9 us
    unnamed x6, local copies, waits for them, and re-layouts  41.2 us
    all_to_all x3, local copies, waits for them, and re-layouts, per_device(): lax.all_to_all(tensor, 'wa', split_axis=3, concat_axis=2, tiled=True)  31.9 us
    dot_general x4, matrix products, per_device(): image = jnp.dot(gram, basis, precision=lax.Precision.HIGHEST)  21.9 us
    dot_general x1, matrix products, per_device(): jnp.einsum('szay,szby->ab', regrouped, regrouped, precision=lax.Precision...  17.8 us
  transfers between devices with their start and end apart: 1, of which 1 were waited for; matrix products, arithmetic and copies ran while one was open for 0% of the time, Pallas kernels for 0%

commit v1 on v0

v1 whole, which is shorter than its diff:
```python
import functools

import jax
import jax.numpy as jnp
from jax import lax
from jax.experimental import pallas as pl
from jax.experimental.pallas import tpu as pltpu
from jax.sharding import PartitionSpec as P

MESH = pl.DeviceIdType.MESH
ITERS = 4
NX = 1024
RANK = 128
KX, KY, KZ = 4, 4, 8
NWA = KX * KZ
PLANES = 32
CHUNKS = 4
PAIRS = [(0, 0), (0, 1), (1, 1), (0, 2), (1, 2), (2, 2), (0, 3), (1, 3), (2, 3), (3, 3)]
BLOCKS = 12
SLOT = [0, 1, 2, 4, 5, 6, 8, 9, 10, 11]
F32, BF16 = jnp.float32, jnp.bfloat16
NT = (((1,), (1,)), ((), ()))


def split(values):
    high = values.astype(BF16)
    return high, (values - high.astype(F32)).astype(BF16)


def pack_tile(loaded, packed, chunk, quad):
    lane = lax.broadcasted_iota(jnp.int32, (8, 128), 1)
    low_half = lane < 64
    even_quarter = lax.rem(lane, 64) < 32
    for group in range(8):
        columns = pl.ds(128 * group, 128)
        v = [loaded[chunk, 4 * quad + m, :, columns] for m in range(4)]
        a = [None] * 4
        for m in range(2):
            a[m] = jnp.where(low_half, v[m], pltpu.roll(v[m + 2], 64, 1))
            a[m + 2] = jnp.where(low_half, pltpu.roll(v[m], 64, 1), v[m + 2])
        out = []
        for m in (0, 2):
            out.append(jnp.where(even_quarter, a[m], pltpu.roll(a[m + 1], 32, 1)))
            out.append(jnp.where(even_quarter, pltpu.roll(a[m], 96, 1), a[m + 1]))
        for m in range(4):
            packed[chunk, 4 * group + m, :, pl.ds(pl.multiple_of(128 * quad, 128), 128)] = out[m]


def regroup_kernel(tensor, high, low, gram, loaded, packed, landed, load_sem, send_sem, recv_sem):
    me = lax.axis_index("wa")

    def peer(step):
        return lax.rem(me + step, NWA)

    def load(chunk):
        return pltpu.make_async_copy(
            tensor.at[:, pl.ds(8 * chunk, 8), :], loaded.at[chunk], load_sem.at[chunk]
        )

    for chunk in range(CHUNKS):
        load(chunk).start()
    barrier = pltpu.get_barrier_semaphore()

    @pl.loop(1, NWA)
    def _(step):
        pl.semaphore_signal(barrier, inc=1, device_id={"wa": peer(step)}, device_id_type=MESH)

    pl.semaphore_wait(barrier, NWA - 1)

    for chunk in range(CHUNKS):
        load(chunk).wait()

        @pl.loop(0, PLANES // 4)
        def _(quad):
            pack_tile(loaded, packed, chunk, quad)

        @pl.loop(1, NWA)
        def _(step):
            to = peer(step)
            pltpu.make_async_remote_copy(
                src_ref=packed.at[chunk, to],
                dst_ref=landed.at[chunk, me],
                send_sem=send_sem.at[chunk],
                recv_sem=recv_sem.at[chunk],
                device_id={"wa": to},
                device_id_type=MESH,
            ).start()

        landed[chunk, me] = packed[chunk, me]

    for chunk in range(CHUNKS):
        others = landed.at[chunk, pl.ds(0, NWA - 1)]
        pltpu.make_async_copy(others, others, recv_sem.at[chunk]).wait()
        rows = pl.ds(256 * chunk, 256)
        high[rows, :], low[rows, :] = split(landed[chunk].reshape(256, NX))
        for slot, (b, c) in zip(SLOT, PAIRS):
            if c != chunk:
                continue
            hb, lb = high[pl.ds(256 * b, 256), :], low[pl.ds(256 * b, 256), :]
            hc, lc = high[rows, :], low[rows, :]
            dot = functools.partial(lax.dot_general, dimension_numbers=NT, preferred_element_type=F32)
            block = dot(hb, hc) + (dot(hb, lc) + dot(lb, hc))
            gram[slot, 0] = block[:, :128]
            gram[slot, 1] = block[:, 128:]
    for slot in (3, 7):
        gram[slot] = jnp.zeros((2, 256, 128), F32)
    for chunk in range(CHUNKS):
        others = packed.at[chunk, pl.ds(0, NWA - 1)]
        pltpu.make_async_copy(others, others, send_sem.at[chunk]).wait()


def regroup(tensor):
    return pl.pallas_call(
        regroup_kernel,
        out_shape=(
            jax.ShapeDtypeStruct((NX, NX), BF16),
            jax.ShapeDtypeStruct((NX, NX), BF16),
            jax.ShapeDtypeStruct((BLOCKS, 2, 256, 128), F32),
        ),
        in_specs=[pl.BlockSpec(memory_space=pl.ANY)],
        out_specs=(pl.BlockSpec(memory_space=pltpu.VMEM),) * 3,
        scratch_shapes=[
            pltpu.VMEM((CHUNKS, PLANES, 8, NX), F32),
            pltpu.VMEM((CHUNKS, NWA, 8, NX), F32),
            pltpu.VMEM((CHUNKS, NWA, 8, NX), F32),
            pltpu.SemaphoreType.DMA((CHUNKS,)),
            pltpu.SemaphoreType.DMA((CHUNKS,)),
            pltpu.SemaphoreType.DMA((CHUNKS,)),
        ],
        compiler_params=pltpu.CompilerParams(
            collective_id=0, has_side_effects=True, vmem_limit_bytes=48 * 1024 * 1024
        ),
        name="regroup_gram",
    )(tensor)


def reduce_kernel(gram, out, from_core, mine, from_xy, sums, from_z, final, gathered, part, sem):
    wa, gz = lax.axis_index("wa"), lax.axis_index("gz")
    x, z = wa // KZ, lax.rem(wa, KZ)
    y, core = gz // 2, lax.rem(gz, 2)
    me_xy = x * KY + y
    other = 1 - core

    def xy_peer(step):
        q = lax.rem(me_xy + step, KX * KY)
        return q, {"wa": (q // KY) * KZ + z, "gz": lax.rem(q, KY) * 2 + core}

    def z_peer(step):
        q = lax.rem(z + step, KZ)
        return q, {"wa": x * KZ + q}

    def send(src, dst, k, device):
        pltpu.make_async_remote_copy(
            src_ref=src, dst_ref=dst, send_sem=sem.at[0, k], recv_sem=sem.at[1, k],
            device_id=device, device_id_type=MESH,
        ).start()

    def wait(ref, k):
        pltpu.make_async_copy(ref, ref, sem.at[1, k]).wait()

    def wait_sent(ref, k):
        pltpu.make_async_copy(ref, ref, sem.at[0, k]).wait()

    barrier = pltpu.get_barrier_semaphore()
    pl.semaphore_signal(barrier, inc=1, device_id={"gz": y * 2 + other}, device_id_type=MESH)

    @pl.loop(1, KX * KY)
    def _(step):
        pl.semaphore_signal(barrier, inc=1, device_id=xy_peer(step)[1], device_id_type=MESH)

    @pl.loop(1, KZ)
    def _(step):
        pl.semaphore_signal(barrier, inc=1, device_id=z_peer(step)[1], device_id_type=MESH)

    pl.semaphore_wait(barrier, 1 + KX * KY - 1 + KZ - 1)

    send(gram.at[:, other], from_core, 0, {"gz": y * 2 + other})
    wait(from_core, 0)
    for b in range(BLOCKS):
        both = gram[b, core] + from_core[b]
        mine[:, b] = both.reshape(16, 16, 128)

    @pl.loop(1, KX * KY)
    def _(step):
        q, device = xy_peer(step)
        send(mine.at[q], from_xy.at[me_xy], 1, device)

    from_xy[me_xy] = mine[me_xy]
    wait(from_xy.at[pl.ds(0, 15)], 1)
    total = from_xy[0]
    for q in range(1, 16):
        total = total + from_xy[q]
    sums[...] = total.reshape(KZ, BLOCKS * 2, 128)

    @pl.loop(1, KZ)
    def _(step):
        q, device = z_peer(step)
        send(sums.at[q], from_z.at[z], 2, device)

    from_z[z] = sums[z]
    wait(from_z.at[pl.ds(0, KZ - 1)], 2)
    total = from_z[0]
    for q in range(1, KZ):
        total = total + from_z[q]
    final[...] = total
    gathered[z] = total

    @pl.loop(1, KZ)
    def _(step):
        q, device = z_peer(step)
        send(final, gathered.at[z], 3, device)

    wait(gathered.at[pl.ds(0, KZ - 1)], 3)
    rows = pl.ds(pl.multiple_of(16 * me_xy, 16), 16)
    part[...] = gathered[...].reshape(BLOCKS, 16, 128)

    @pl.loop(1, KX * KY)
    def _(step):
        q, device = xy_peer(step)
        send(part, out.at[:, core, rows, :], 4, device)

    out[:, core, rows, :] = part[...]
    wait(out.at[:, 0, pl.ds(0, 240), :], 4)
    send(out.at[:, core], out.at[:, core], 5, {"gz": y * 2 + other})
    wait(out.at[:, other], 5)
    wait_sent(from_core, 0)
    wait_sent(mine.at[pl.ds(0, 15)], 1)
    wait_sent(sums.at[pl.ds(0, KZ - 1)], 2)
    wait_sent(gathered.at[pl.ds(0, KZ - 1)], 3)
    wait_sent(mine.at[pl.ds(0, 15)], 4)
    wait_sent(from_core, 5)


def reduce_gram(gram):
    part = BLOCKS * 2
    return pl.pallas_call(
        reduce_kernel,
        out_shape=jax.ShapeDtypeStruct((BLOCKS, 2, 256, 128), F32),
        in_specs=[pl.BlockSpec(memory_space=pltpu.VMEM)],
        out_specs=pl.BlockSpec(memory_space=pltpu.VMEM),
        scratch_shapes=[
            pltpu.VMEM((BLOCKS, 256, 128), F32),
            pltpu.VMEM((16, BLOCKS, 16, 128), F32),
            pltpu.VMEM((16, BLOCKS, 16, 128), F32),
            pltpu.VMEM((KZ, part, 128), F32),
            pltpu.VMEM((KZ, part, 128), F32),
            pltpu.VMEM((part, 128), F32),
            pltpu.VMEM((KZ, part, 128), F32),
            pltpu.VMEM((BLOCKS, 16, 128), F32),
            pltpu.SemaphoreType.DMA((2, 6)),
        ],
        compiler_params=pltpu.CompilerParams(
            collective_id=1, has_side_effects=True, vmem_limit_bytes=40 * 1024 * 1024
        ),
        name="reduce_gram",
    )(gram)


def inverse_factor(small, lower_inv):
    lane = lax.broadcasted_iota(jnp.int32, (8, RANK), 1)
    row_in_tile = lax.broadcasted_iota(jnp.int32, (8, RANK), 0)
    tiles = [small[8 * t : 8 * t + 8, :] for t in range(RANK // 8)]
    for j in range(RANK):
        t, s = divmod(j, 8)
        spread = {u: jnp.broadcast_to(tiles[u][:, j : j + 1], (8, RANK)) for u in range(t, RANK // 8)}
        pivot = jnp.broadcast_to(spread[t][s : s + 1, :], (8, RANK))
        row = jnp.broadcast_to(tiles[t][s : s + 1, :], (8, RANK))
        row = jnp.where(lane == j, 1.0, row)
        scaled = row * (1.0 / pivot)
        root = lax.rsqrt(pivot)
        lower_inv[j : j + 1, :] = jnp.where(lane <= j, row * root, 0.0)[0:1, :]
        for u in range(t, RANK // 8):
            kept = jnp.where(lane == j, 0.0, tiles[u])
            changed = kept - spread[u] * scaled
            tiles[u] = jnp.where(row_in_tile > s, changed, tiles[u]) if u == t else changed
    return None


def factor_kernel(gram, start, high, low, factor, core, gram_high, gram_low, basis_ref, image_ref, lower_inv):
    scale = 1.0 / 262144
    for slot, (b, c) in zip(SLOT, PAIRS):
        block = jnp.concatenate([gram[slot, 0], gram[slot, 1]], axis=1) * scale
        rb, rc = pl.ds(256 * b, 256), pl.ds(256 * c, 256)
        if b == c:
            gram_high[rb, rc], gram_low[rb, rc] = split(block)
        else:
            gram_high[rb, rc], gram_low[rb, rc] = split(block)
            gram_high[rc, rb], gram_low[rc, rb] = split(block.T)
    for c in range(CHUNKS):
        basis_ref[pl.ds(256 * c, 256), :] = start[:, c].reshape(256, RANK)

    @pl.loop(0, ITERS)
    def _(step):
        bh, bl = split(basis_ref[...])
        both = jnp.concatenate([bh, bl], axis=1)
        for c in range(CHUNKS):
            rows = pl.ds(256 * c, 256)
            wide = jnp.dot(gram_high[rows, :], both, preferred_element_type=F32)
            cross = jnp.dot(gram_low[rows, :], bh, preferred_element_type=F32)
            image_ref[rows, :] = wide[:, :RANK] + (wide[:, RANK:] + cross)
        image = image_ref[...]
        small = lax.dot_general(
            image, image, (((0,), (0,)), ((), ())), precision=lax.Precision.HIGHEST, preferred_element_type=F32
        )
        inverse_factor(small, lower_inv)
        basis_ref[...] = lax.dot_general(
            image, lower_inv[...], NT, precision=lax.Precision.HIGHEST, preferred_element_type=F32
        )

    basis = basis_ref[...]
    for c in range(CHUNKS):
        factor[:, c] = basis[256 * c : 256 * c + 256].reshape(NWA, 8, RANK)
    fh, fl = split(basis.T)
    both = jnp.concatenate([fh, fl], axis=0)
    for q in range(8):
        columns = pl.ds(128 * q, 128)
        wide = jnp.dot(both, high[:, columns], preferred_element_type=F32)
        cross = jnp.dot(fh, low[:, columns], preferred_element_type=F32)
        tile = wide[:RANK] + (wide[RANK:] + cross)
        for m in range(4):
            core[4 * q + m] = tile[:, 32 * m : 32 * m + 32]


def factor_and_core(gram, start, high, low):
    return pl.pallas_call(
        factor_kernel,
        out_shape=(
            jax.ShapeDtypeStruct((NWA, CHUNKS, 8, RANK), F32),
            jax.ShapeDtypeStruct((PLANES, RANK, 32), F32),
        ),
        in_specs=[pl.BlockSpec(memory_space=pltpu.VMEM)] * 4,
        out_specs=(pl.BlockSpec(memory_space=pltpu.VMEM),) * 2,
        scratch_shapes=[
            pltpu.VMEM((NX, NX), BF16),
            pltpu.VMEM((NX, NX), BF16),
            pltpu.VMEM((NX, RANK), F32),
            pltpu.VMEM((NX, RANK), F32),
            pltpu.VMEM((RANK, RANK), F32),
        ],
        compiler_params=pltpu.CompilerParams(vmem_limit_bytes=48 * 1024 * 1024),
        name="factor_core",
    )(gram, start, high, low)


def per_device(tensor, start):
    high, low, gram = regroup(tensor.reshape(PLANES, 32, NX))
    gram = reduce_gram(gram)
    factor, core = factor_and_core(gram, start.reshape(NWA, CHUNKS, 8, RANK), high, low)
    return factor.reshape(NX, RANK), core.reshape(4, 8, RANK, 32)


def solution(mesh):
    placed = (P(None, "gz", "wa", None), P())
    return jax.shard_map(
        per_device,
        mesh=mesh,
        in_specs=placed,
        out_specs=(P(), P(None, "gz", None, "wa")),
        check_vma=False,
    )
```

time: 627 us -> 266 us (0.42)
  waiting for transfers between devices: 268 us -> 0 us
  Pallas kernels: 0 us -> 255 us
  other arithmetic: 105 us -> 0 us
  blocking collectives: 104 us -> 0 us
  local copies, waits for them, and re-layouts: 73.5 us -> 6.25 us
  matrix products: 52.7 us -> 0 us
  between operations: 14.7 us -> 0.67 us
    psum x1 -> x0, waiting for transfers between devices: 268 us -> none  [per_device(): gram = lax.psum(local_gram, ('wa', 'gz'))]
    pallas_call x0 -> x3, Pallas kernels: none -> 255 us  [the longest x1 106 us: regroup(): pl.pallas_call(regroup_kernel, out_shape=(jax.ShapeDtypeStruct((NX, NX),...]
    all_to_all x1 -> x0, blocking collectives: 104 us -> none  [per_device(): lax.all_to_all(tensor, 'wa', split_axis=3, concat_axis=2, tiled=True)]
    another operation x20 -> x0, other arithmetic: 91.4 us -> none  [the longest x12 49.6 us: orthonormal(): lower = jnp.linalg.cholesky(small)]
    dot_general x10 -> x0, matrix products: 50.1 us -> none  [the longest x4 21.9 us: per_device(): image = jnp.dot(gram, basis, precision=lax.Precision.HIGHEST)]
    unnamed x6 -> x9, local copies, waits for them, and re-layouts: 41.2 us -> 6.25 us
    all_to_all x3 -> x0, local copies, waits for them, and re-layouts: 31.9 us -> none  [per_device(): lax.all_to_all(tensor, 'wa', split_axis=3, concat_axis=2, tiled=True)]
    all_to_all x1 -> x0, other arithmetic: 13.7 us -> none  [per_device(): lax.all_to_all(tensor, 'wa', split_axis=3, concat_axis=2, tiled=True)]
  transfers between devices with their start and end apart: 1 -> 0, of which waited for: 1 -> 0; matrix products, arithmetic and copies ran while one was open for 0% -> 0% of each run, Pallas kernels for 0% -> 0%
where the time goes in v1:
time: 266 us; the launch traced here: 262 us
  Pallas kernels  255 us (96%)
  local copies, waits for them, and re-layouts  6.25 us (2%)
    pallas_call x1, Pallas kernels, regroup(): pl.pallas_call(regroup_kernel, out_shape=(jax.ShapeDtypeStruct((NX, NX),...  106 us
    pallas_call x1, Pallas kernels, factor_and_core(): pl.pallas_call(factor_kernel, out_shape=(jax.ShapeDtypeStruct((NWA, CHUNK...  83.5 us
    pallas_call x1, Pallas kernels, reduce_gram(): pl.pallas_call(reduce_kernel, out_shape=jax.ShapeDtypeStruct((BLOCKS, 2,...  65.5 us
    unnamed x9, local copies, waits for them, and re-layouts  6.25 us

profile of v1, /device:TPU:1, one launch (start us, length us, event | category | flops | bytes accessed | tf_op | source)
XLA Modules:
  0.0 262.2 jit_solution(8116407731361457485)
XLA Ops:
  0.6 106.3 %regroup_gram.1 = (bf16[1024,1024]{1,0:T(8,128)(2,1)S(1)}, bf16[1024,1024]{1,0:T(8,128)(2,1)S(1)}, f32[12,2,256,128]{3,2,1,0:T(8,128)}) custom-call(f32[32,32,1024]{2,1,0:T(8,128)} %bitcast.6), custom_call_target="tpu_custom_call" | custom-call | tf_op jit(solution)/shard_map/regroup_gram/pallas_call | solution.py:113
  106.9 0.0 copy-start.2
  106.9 1.3 copy-done.2
  108.3 0.0 copy-start.1
  108.3 1.9 copy-done.1
  110.2 0.0 copy-start.3
  110.2 65.5 %reduce_gram.1.gram = f32[12,2,256,128]{3,2,1,0:T(8,128)S(1)} custom-call(f32[12,2,256,128]{3,2,1,0:T(8,128)S(1)} %copy-done.1), custom_call_target="tpu_custom_call" | custom-call | tf_op jit(solution)/shard_map/reduce_gram/pallas_call | solution.py:236
  175.7 0.0 copy-start
  175.7 1.6 copy-done
  177.3 0.0 copy-done.3
  177.3 83.5 %factor_core.1 = (f32[32,4,8,128]{3,2,1,0:T(8,128)}, f32[32,128,32]{2,1,0:T(8,128)S(1)}) custom-call(f32[12,2,256,128]{3,2,1,0:T(8,128)} %copy-done, f32[32,4,8,128]{3,2,1,0:T(8,128)S(1)} %bitcast.5, bf16[1024,1024]{1,0:T(8,128)(2,1)S(1)} %get-tuple-element.8.high, bf16[1024,1024]{1,0:T(8,128)(2,1)} %copy-done.2), custom_call_target="tpu_custom_call" | custom-call | tf_op jit(solution)/shard_map/factor_core/pallas_call | solution.py:325
  260.9 1.4 copy.4
Async XLA Ops:
  106.9 1.3 copy-start.2
  108.3 1.9 copy-start.1
  110.2 67.2 %copy-start.3 = (f32[1024,128]{1,0:T(8,128)S(1)}, f32[1024,128]{1,0:T(8,128)}, u32[]{:S(2)}) copy-start(f32[1024,128]{1,0:T(8,128)} %param.3) | copy-start | bytes 1572868
  175.7 1.7 copy-start

commit v2 on v0

v2 whole, which is shorter than its diff:
```python
import functools

import jax
import jax.numpy as jnp
from jax import lax
from jax.experimental import pallas as pl
from jax.experimental.pallas import tpu as pltpu
from jax.sharding import PartitionSpec as P

MESH = pl.DeviceIdType.MESH
ITERS = 4
NX = 1024
RANK = 128
KX, KY, KZ = 4, 4, 8
NWA = KX * KZ
PLANES = 32
CHUNKS = 4
ROUNDS = [
    [(0, 0), (0, 1), (1, 1)],
    [(0, 2), (1, 2), (2, 2)],
    [(0, 3), (1, 3), (2, 3), (3, 3)],
]
SLOTS = 4
NXY = KX * KY
TILES = SLOTS * 2
F32, BF16 = jnp.float32, jnp.bfloat16
NT = (((1,), (1,)), ((), ()))


def split(values):
    high = values.astype(BF16)
    return high, (values - high.astype(F32)).astype(BF16)


def pack_tile(loaded, packed, chunk, quad):
    lane = lax.broadcasted_iota(jnp.int32, (8, 128), 1)
    low_half = lane < 64
    even_quarter = lax.rem(lane, 64) < 32
    for group in range(8):
        columns = pl.ds(128 * group, 128)
        v = [loaded[chunk, 4 * quad + m, :, columns] for m in range(4)]
        a = [None] * 4
        for m in range(2):
            a[m] = jnp.where(low_half, v[m], pltpu.roll(v[m + 2], 64, 1))
            a[m + 2] = jnp.where(low_half, pltpu.roll(v[m], 64, 1), v[m + 2])
        out = []
        for m in (0, 2):
            out.append(jnp.where(even_quarter, a[m], pltpu.roll(a[m + 1], 32, 1)))
            out.append(jnp.where(even_quarter, pltpu.roll(a[m], 96, 1), a[m + 1]))
        for m in range(4):
            packed[chunk, 4 * group + m, :, pl.ds(pl.multiple_of(128 * quad, 128), 128)] = out[m]


def inverse_factor(small, lower_inv):
    lane = lax.broadcasted_iota(jnp.int32, (8, RANK), 1)
    full = (8, RANK)
    count = RANK // 8
    tiles = [small[8 * t : 8 * t + 8, :] for t in range(count)]

    def columns(u, t):
        return [jnp.broadcast_to(tiles[u][:, 8 * t + s : 8 * t + s + 1], full) for s in range(8)]

    def spread(t):
        cols = columns(t, t)
        entry = {(i, s): jnp.broadcast_to(cols[s][i : i + 1, :], full) for s in range(8) for i in range(s, 8)}
        rows = []
        for s in range(8):
            row = jnp.broadcast_to(tiles[t][s : s + 1, :], full)
            inside = (lane >= 8 * t) & (lane < 8 * t + 8)
            rows.append(jnp.where(inside, jnp.where(lane == 8 * t + s, 1.0, 0.0), row))
        return entry, rows

    def update(u, t, lower, root, rows):
        cols = columns(u, t)
        inside = (lane >= 8 * t) & (lane < 8 * t + 8)
        tile = jnp.where(inside, 0.0, tiles[u])
        for k in range(8):
            cols[k] = cols[k] * root[k]
            for i in range(k + 1, 8):
                cols[i] = cols[i] - lower[i, k] * cols[k]
            tile = tile - cols[k] * rows[k]
        tiles[u] = tile

    entry, rows = spread(0)
    for t in range(count):
        root, lower = [], {}
        for k in range(8):
            root.append(lax.rsqrt(entry[k, k]))
            for i in range(k + 1, 8):
                lower[i, k] = entry[i, k] * root[k]
            for i in range(k + 1, 8):
                for j in range(k + 1, i + 1):
                    entry[i, j] = entry[i, j] - lower[i, k] * lower[j, k]
            rows[k] = rows[k] * root[k]
            for i in range(k + 1, 8):
                rows[i] = rows[i] - lower[i, k] * rows[k]
        done = rows
        if t + 1 < count:
            update(t + 1, t, lower, root, done)
            entry, rows = spread(t + 1)
        for u in range(t + 2, count):
            update(u, t, lower, root, done)
        for k in range(8):
            j = 8 * t + k
            lower_inv[j : j + 1, :] = jnp.where(lane <= j, done[k], 0.0)[0:1, :]


def kernel(
    tensor, start, factor, core_out,
    loaded, packed, landed, high, low,
    gram, from_core, mine, from_xy, sums, from_z, final, gathered, part, whole,
    gram_high, gram_low, basis_ref, image_ref, lower_inv,
    load_sem, send_sem, recv_sem, sem,
):
    me, gz = lax.axis_index("wa"), lax.axis_index("gz")
    x, z = me // KZ, lax.rem(me, KZ)
    y, core = gz // 2, lax.rem(gz, 2)
    me_xy = x * KY + y
    other = 1 - core
    sibling = {"gz": y * 2 + other}

    def peer(step):
        return lax.rem(me + step, NWA)

    def xy_peer(step):
        q = lax.rem(me_xy + step, NXY)
        return q, {"wa": (q // KY) * KZ + z, "gz": lax.rem(q, KY) * 2 + core}

    def z_peer(step):
        q = lax.rem(z + step, KZ)
        return q, {"wa": x * KZ + q}

    def load(chunk):
        return pltpu.make_async_copy(
            tensor.at[:, pl.ds(8 * chunk, 8), :], loaded.at[chunk], load_sem.at[chunk]
        )

    for chunk in range(CHUNKS):
        load(chunk).start()
    barrier = pltpu.get_barrier_semaphore()

    def greet(device):
        pl.semaphore_signal(barrier, inc=1, device_id=device, device_id_type=MESH)

    @pl.loop(1, NWA)
    def _(step):
        greet({"wa": peer(step)})

    @pl.loop(1, NXY)
    def _(step):
        greet(xy_peer(step)[1])

    greet(sibling)
    pl.semaphore_wait(barrier, NWA - 1 + NXY - 1 + 1)

    def pack(chunk):
        load(chunk).wait()

        @pl.loop(0, PLANES // 4)
        def _(quad):
            pack_tile(loaded, packed, chunk, quad)

    def send_chunk(chunk):
        @pl.loop(1, NWA)
        def _(step):
            to = peer(step)
            pltpu.make_async_remote_copy(
                src_ref=packed.at[chunk, to],
                dst_ref=landed.at[chunk, me],
                send_sem=send_sem.at[chunk],
                recv_sem=recv_sem.at[chunk],
                device_id={"wa": to},
                device_id_type=MESH,
            ).start()

        landed[chunk, me] = packed[chunk, me]

    def take_chunk(chunk):
        others = landed.at[chunk, pl.ds(0, NWA - 1)]
        pltpu.make_async_copy(others, others, recv_sem.at[chunk]).wait()
        rows = pl.ds(256 * chunk, 256)
        high[rows, :], low[rows, :] = split(landed[chunk].reshape(256, NX))

    def multiply(r, chunk):
        dot = functools.partial(lax.dot_general, dimension_numbers=NT, preferred_element_type=F32)
        for slot, (b, c) in enumerate(ROUNDS[r]):
            if c != chunk:
                continue
            hb, lb = high[pl.ds(256 * b, 256), :], low[pl.ds(256 * b, 256), :]
            hc, lc = high[pl.ds(256 * c, 256), :], low[pl.ds(256 * c, 256), :]
            block = dot(hb, hc) + (dot(hb, lc) + dot(lb, hc))
            gram[r, slot, 0] = block[:, :128]
            gram[r, slot, 1] = block[:, 128:]

    def send(src, dst, r, k, device):
        pltpu.make_async_remote_copy(
            src_ref=src, dst_ref=dst, send_sem=sem.at[0, r, k], recv_sem=sem.at[1, r, k],
            device_id=device, device_id_type=MESH,
        ).start()

    def wait(ref, r, k, way=1):
        pltpu.make_async_copy(ref, ref, sem.at[way, r, k]).wait()

    share = pl.ds(pl.multiple_of(16 * me_xy, 16), 16)

    def to_core(r):
        for slot in range(len(ROUNDS[r]), SLOTS):
            gram[r, slot] = jnp.zeros((2, 256, 128), F32)
        send(gram.at[r, :, other], from_core.at[r], r, 0, sibling)

    def to_xy(r):
        wait(from_core.at[r], r, 0)
        for slot in range(SLOTS):
            mine[r, :, slot] = (gram[r, slot, core] + from_core[r, slot]).reshape(NXY, 16, 128)

        @pl.loop(1, NXY)
        def _(step):
            q, device = xy_peer(step)
            send(mine.at[r, q], from_xy.at[r, me_xy], r, 1, device)

        from_xy[r, me_xy] = mine[r, me_xy]

    def to_z(r):
        wait(from_xy.at[r, pl.ds(0, NXY - 1)], r, 1)
        total = from_xy[r, 0]
        for q in range(1, NXY):
            total = total + from_xy[r, q]
        sums[r] = total.reshape(KZ, TILES, 128)

        @pl.loop(1, KZ)
        def _(step):
            q, device = z_peer(step)
            send(sums.at[r, q], from_z.at[r, z], r, 2, device)

        from_z[r, z] = sums[r, z]

    def back_z(r):
        wait(from_z.at[r, pl.ds(0, KZ - 1)], r, 2)
        total = from_z[r, 0]
        for q in range(1, KZ):
            total = total + from_z[r, q]
        final[r] = total
        gathered[r, z] = total

        @pl.loop(1, KZ)
        def _(step):
            q, device = z_peer(step)
            send(final.at[r], gathered.at[r, z], r, 3, device)

    def back_xy(r):
        wait(gathered.at[r, pl.ds(0, KZ - 1)], r, 3)
        part[r] = gathered[r].reshape(SLOTS, 16, 128)

        @pl.loop(1, NXY)
        def _(step):
            q, device = xy_peer(step)
            send(part.at[r], whole.at[r, :, core, share, :], r, 4, device)

        whole[r, :, core, share, :] = part[r]

    def back_core(r):
        wait(whole.at[r, :, 0, pl.ds(0, 240), :], r, 4)
        send(whole.at[r, :, core], whole.at[r, :, core], r, 5, sibling)

    def finish(r):
        wait(whole.at[r, :, other], r, 5)
        for slot, (b, c) in enumerate(ROUNDS[r]):
            block = jnp.concatenate([whole[r, slot, 0], whole[r, slot, 1]], axis=1) * (1.0 / 262144)
            rb, rc = pl.ds(256 * b, 256), pl.ds(256 * c, 256)
            gram_high[rb, rc], gram_low[rb, rc] = split(block)
            if b != c:
                gram_high[rc, rb], gram_low[rc, rb] = split(block.T)

    for chunk in range(CHUNKS):
        pack(chunk)
        send_chunk(chunk)
    take_chunk(0)
    multiply(0, 0)
    take_chunk(1)
    multiply(0, 1)
    to_core(0)
    to_xy(0)
    to_z(0)
    back_z(0)
    back_xy(0)
    take_chunk(2)
    multiply(1, 2)
    to_core(1)
    back_core(0)
    to_xy(1)
    finish(0)
    to_z(1)
    back_z(1)
    back_xy(1)
    take_chunk(3)
    multiply(2, 3)
    to_core(2)
    to_xy(2)
    back_core(1)
    finish(1)
    to_z(2)
    back_z(2)
    back_xy(2)
    back_core(2)
    finish(2)

    for c in range(CHUNKS):
        basis_ref[pl.ds(256 * c, 256), :] = start[:, c].reshape(256, RANK)

    @pl.loop(0, ITERS)
    def _(step):
        bh, bl = split(basis_ref[...])
        both = jnp.concatenate([bh, bl], axis=1)
        for c in range(CHUNKS):
            rows = pl.ds(256 * c, 256)
            wide = jnp.dot(gram_high[rows, :], both, preferred_element_type=F32)
            cross = jnp.dot(gram_low[rows, :], bh, preferred_element_type=F32)
            image_ref[rows, :] = wide[:, :RANK] + (wide[:, RANK:] + cross)
        image = image_ref[...]
        small = lax.dot_general(
            image, image, (((0,), (0,)), ((), ())), precision=lax.Precision.HIGHEST, preferred_element_type=F32
        )
        inverse_factor(small, lower_inv)
        basis_ref[...] = lax.dot_general(
            image, lower_inv[...], NT, precision=lax.Precision.HIGHEST, preferred_element_type=F32
        )

    basis = basis_ref[...]
    for c in range(CHUNKS):
        factor[:, c] = basis[256 * c : 256 * c + 256].reshape(NWA, 8, RANK)
    fh, fl = split(basis.T)
    both = jnp.concatenate([fh, fl], axis=0)
    for q in range(8):
        columns = pl.ds(128 * q, 128)
        wide = jnp.dot(both, high[:, columns], preferred_element_type=F32)
        cross = jnp.dot(fh, low[:, columns], preferred_element_type=F32)
        tile = wide[:RANK] + (wide[RANK:] + cross)
        for m in range(4):
            core_out[4 * q + m] = tile[:, 32 * m : 32 * m + 32]

    for chunk in range(CHUNKS):
        others = packed.at[chunk, pl.ds(0, NWA - 1)]
        pltpu.make_async_copy(others, others, send_sem.at[chunk]).wait()
    for r in range(len(ROUNDS)):
        wait(from_core.at[r], r, 0, 0)
        wait(mine.at[r, pl.ds(0, NXY - 1)], r, 1, 0)
        wait(sums.at[r, pl.ds(0, KZ - 1)], r, 2, 0)
        wait(gathered.at[r, pl.ds(0, KZ - 1)], r, 3, 0)
        wait(mine.at[r, pl.ds(0, NXY - 1)], r, 4, 0)
        wait(from_core.at[r], r, 5, 0)


def per_device(tensor, start):
    n = len(ROUNDS)
    factor, core = pl.pallas_call(
        kernel,
        out_shape=(
            jax.ShapeDtypeStruct((NWA, CHUNKS, 8, RANK), F32),
            jax.ShapeDtypeStruct((PLANES, RANK, 32), F32),
        ),
        in_specs=[pl.BlockSpec(memory_space=pl.ANY), pl.BlockSpec(memory_space=pltpu.VMEM)],
        out_specs=(pl.BlockSpec(memory_space=pltpu.VMEM),) * 2,
        scratch_shapes=[
            pltpu.VMEM((CHUNKS, PLANES, 8, NX), F32),
            pltpu.VMEM((CHUNKS, NWA, 8, NX), F32),
            pltpu.VMEM((CHUNKS, NWA, 8, NX), F32),
            pltpu.VMEM((NX, NX), BF16),
            pltpu.VMEM((NX, NX), BF16),
            pltpu.VMEM((n, SLOTS, 2, 256, 128), F32),
            pltpu.VMEM((n, SLOTS, 256, 128), F32),
            pltpu.VMEM((n, NXY, SLOTS, 16, 128), F32),
            pltpu.VMEM((n, NXY, SLOTS, 16, 128), F32),
            pltpu.VMEM((n, KZ, TILES, 128), F32),
            pltpu.VMEM((n, KZ, TILES, 128), F32),
            pltpu.VMEM((n, TILES, 128), F32),
            pltpu.VMEM((n, KZ, TILES, 128), F32),
            pltpu.VMEM((n, SLOTS, 16, 128), F32),
            pltpu.VMEM((n, SLOTS, 2, 256, 128), F32),
            pltpu.VMEM((NX, NX), BF16),
            pltpu.VMEM((NX, NX), BF16),
            pltpu.VMEM((NX, RANK), F32),
            pltpu.VMEM((NX, RANK), F32),
            pltpu.VMEM((RANK, RANK), F32),
            pltpu.SemaphoreType.DMA((CHUNKS,)),
            pltpu.SemaphoreType.DMA((CHUNKS,)),
            pltpu.SemaphoreType.DMA((CHUNKS,)),
            pltpu.SemaphoreType.DMA((2, n, 6)),
        ],
        compiler_params=pltpu.CompilerParams(
            collective_id=0, has_side_effects=True, vmem_limit_bytes=56 * 1024 * 1024
        ),
        name="factor_core",
    )(tensor.reshape(PLANES, 32, NX), start.reshape(NWA, CHUNKS, 8, RANK))
    return factor.reshape(NX, RANK), core.reshape(4, 8, RANK, 32)


def solution(mesh):
    placed = (P(None, "gz", "wa", None), P())
    return jax.shard_map(
        per_device,
        mesh=mesh,
        in_specs=placed,
        out_specs=(P(), P(None, "gz", None, "wa")),
        check_vma=False,
    )
```

time: 627 us -> 205 us (0.33); the launches traced: 618 us -> 205 us
  waiting for transfers between devices: 268 us -> 0 us
  Pallas kernels: 0 us -> 199 us
  other arithmetic: 105 us -> 0 us
  blocking collectives: 104 us -> 0 us
  local copies, waits for them, and re-layouts: 73.5 us -> 4.83 us
  matrix products: 52.7 us -> 0 us
  between operations: 14.7 us -> 0.64 us
    psum x1 -> x0, waiting for transfers between devices: 268 us -> none  [per_device(): gram = lax.psum(local_gram, ('wa', 'gz'))]
    pallas_call x0 -> x1, Pallas kernels: none -> 199 us  [per_device(): pl.pallas_call(kernel, out_shape=(jax.ShapeDtypeStruct((NWA, CHUNKS, 8, R...]
    all_to_all x1 -> x0, blocking collectives: 104 us -> none  [per_device(): lax.all_to_all(tensor, 'wa', split_axis=3, concat_axis=2, tiled=True)]
    another operation x20 -> x0, other arithmetic: 91.4 us -> none  [the longest x12 49.6 us: orthonormal(): lower = jnp.linalg.cholesky(small)]
    dot_general x10 -> x0, matrix products: 50.1 us -> none  [the longest x4 21.9 us: per_device(): image = jnp.dot(gram, basis, precision=lax.Precision.HIGHEST)]
    unnamed x6 -> x2, local copies, waits for them, and re-layouts: 41.2 us -> 4.83 us
    all_to_all x3 -> x0, local copies, waits for them, and re-layouts: 31.9 us -> none  [per_device(): lax.all_to_all(tensor, 'wa', split_axis=3, concat_axis=2, tiled=True)]
    all_to_all x1 -> x0, other arithmetic: 13.7 us -> none  [per_device(): lax.all_to_all(tensor, 'wa', split_axis=3, concat_axis=2, tiled=True)]
  transfers between devices with their start and end apart: 1 -> 0, of which waited for: 1 -> 0; matrix products, arithmetic and copies ran while one was open for 0% -> 0% of each run, Pallas kernels for 0% -> 0%
where the time goes in v2:
time: 205 us
  Pallas kernels  199 us (97%)
  local copies, waits for them, and re-layouts  4.83 us (2%)
    pallas_call x1, Pallas kernels, per_device(): pl.pallas_call(kernel, out_shape=(jax.ShapeDtypeStruct((NWA, CHUNKS, 8, R...  199 us
    unnamed x2, local copies, waits for them, and re-layouts  4.83 us

profile of v2, /device:TPU:1, one launch (start us, length us, event | category | flops | bytes accessed | tf_op | source)
XLA Modules:
  0.0 204.7 jit_solution(5280615258672559577)
XLA Ops:
  0.6 199.2 %factor_core.1 = (f32[32,4,8,128]{3,2,1,0:T(8,128)}, f32[32,128,32]{2,1,0:T(8,128)}) custom-call(f32[32,32,1024]{2,1,0:T(8,128)} %bitcast.4, f32[32,4,8,128]{3,2,1,0:T(8,128)} %bitcast.6), custom_call_target="tpu_custom_call" | custom-call | tf_op jit(solution)/shard_map/factor_core/pallas_call | solution.py:355
  199.9 3.0 %copy.4 = f32[4,8,128,32]{2,3,1,0:T(8,128)} copy(f32[4,8,128,32]{3,2,1,0:T(8,128)} %bitcast.5) | data formatting | bytes 1048576
  202.8 1.9 copy.6

commit v3 on v2

--- a/solution.py
+++ b/solution.py
@@ -14,6 +14,8 @@
 KX, KY, KZ = 4, 4, 8
 NWA = KX * KZ
 PLANES = 32
+BATCH = 4
+BATCHES = -(-(NWA - 1) // BATCH)
 CHUNKS = 4
 ROUNDS = [
     [(0, 0), (0, 1), (1, 1)],
@@ -160,20 +162,34 @@
         def _(quad):
             pack_tile(loaded, packed, chunk, quad)
 
-    def send_chunk(chunk):
-        @pl.loop(1, NWA)
+    def batch(k):
+        chunk, part = divmod(k, BATCHES)
+        first = 1 + BATCH * part
+        return chunk, part, first, min(first + BATCH, NWA)
+
+    def send_batch(k):
+        chunk, part, first, end = batch(k)
+
+        @pl.loop(first, end)
         def _(step):
-            to = peer(step)
+            half = lax.div(step + 1, 2)
+            to = peer(jnp.where(lax.rem(step, 2) == 1, half, NWA - half))
             pltpu.make_async_remote_copy(
                 src_ref=packed.at[chunk, to],
                 dst_ref=landed.at[chunk, me],
-                send_sem=send_sem.at[chunk],
+                send_sem=send_sem.at[chunk, part],
                 recv_sem=recv_sem.at[chunk],
                 device_id={"wa": to},
                 device_id_type=MESH,
             ).start()
 
-        landed[chunk, me] = packed[chunk, me]
+        if part == 0:
+            landed[chunk, me] = packed[chunk, me]
+
+    def batch_left(k):
+        chunk, part, first, end = batch(k)
+        others = packed.at[chunk, pl.ds(0, end - first)]
+        pltpu.make_async_copy(others, others, send_sem.at[chunk, part]).wait()
 
     def take_chunk(chunk):
         others = landed.at[chunk, pl.ds(0, NWA - 1)]
@@ -204,28 +220,32 @@
     share = pl.ds(pl.multiple_of(16 * me_xy, 16), 16)
 
     def to_core(r):
-        for slot in range(len(ROUNDS[r]), SLOTS):
-            gram[r, slot] = jnp.zeros((2, 256, 128), F32)
-        send(gram.at[r, :, other], from_core.at[r], r, 0, sibling)
+        used = pl.ds(0, len(ROUNDS[r]))
+        send(gram.at[r, used, other], from_core.at[r, used], r, 0, sibling)
 
     def to_xy(r):
-        wait(from_core.at[r], r, 0)
-        for slot in range(SLOTS):
+        used = pl.ds(0, len(ROUNDS[r]))
+        wait(from_core.at[r, used], r, 0)
+        for slot in range(len(ROUNDS[r])):
             mine[r, :, slot] = (gram[r, slot, core] + from_core[r, slot]).reshape(NXY, 16, 128)
 
         @pl.loop(1, NXY)
         def _(step):
             q, device = xy_peer(step)
-            send(mine.at[r, q], from_xy.at[r, me_xy], r, 1, device)
-
-        from_xy[r, me_xy] = mine[r, me_xy]
+            send(mine.at[r, q, used], from_xy.at[r, me_xy, used], r, 1, device)
+
+        from_xy[r, me_xy, used] = mine[r, me_xy, used]
 
     def to_z(r):
-        wait(from_xy.at[r, pl.ds(0, NXY - 1)], r, 1)
-        total = from_xy[r, 0]
+        n = len(ROUNDS[r])
+        used = pl.ds(0, n)
+        wait(from_xy.at[r, pl.ds(0, NXY - 1), used], r, 1)
+        total = from_xy[r, 0, used]
         for q in range(1, NXY):
-            total = total + from_xy[r, q]
-        sums[r] = total.reshape(KZ, TILES, 128)
+            total = total + from_xy[r, q, used]
+        sums[r, pl.ds(0, 2 * n)] = total.reshape(2 * n, TILES, 128)
+        if n < SLOTS:
+            sums[r, pl.ds(2 * n, KZ - 2 * n)] = jnp.zeros((KZ - 2 * n, TILES, 128), F32)
 
         @pl.loop(1, KZ)
         def _(step):
@@ -249,21 +269,24 @@
 
     def back_xy(r):
         wait(gathered.at[r, pl.ds(0, KZ - 1)], r, 3)
-        part[r] = gathered[r].reshape(SLOTS, 16, 128)
+        n = len(ROUNDS[r])
+        used = pl.ds(0, n)
+        part[r, used] = gathered[r, pl.ds(0, 2 * n)].reshape(n, 16, 128)
 
         @pl.loop(1, NXY)
         def _(step):
             q, device = xy_peer(step)
-            send(part.at[r], whole.at[r, :, core, share, :], r, 4, device)
-
-        whole[r, :, core, share, :] = part[r]
+            send(part.at[r, used], whole.at[r, used, core, share, :], r, 4, device)
+
+        whole[r, used, core, share, :] = part[r, used]
 
     def back_core(r):
-        wait(whole.at[r, :, 0, pl.ds(0, 240), :], r, 4)
-        send(whole.at[r, :, core], whole.at[r, :, core], r, 5, sibling)
+        used = pl.ds(0, len(ROUNDS[r]))
+        wait(whole.at[r, used, 0, pl.ds(0, 240), :], r, 4)
+        send(whole.at[r, used, core], whole.at[r, used, core], r, 5, sibling)
 
     def finish(r):
-        wait(whole.at[r, :, other], r, 5)
+        wait(from_core.at[r, pl.ds(0, len(ROUNDS[r]))], r, 5)
         for slot, (b, c) in enumerate(ROUNDS[r]):
             block = jnp.concatenate([whole[r, slot, 0], whole[r, slot, 1]], axis=1) * (1.0 / 262144)
             rb, rc = pl.ds(256 * b, 256), pl.ds(256 * c, 256)
@@ -271,39 +294,103 @@
             if b != c:
                 gram_high[rc, rb], gram_low[rc, rb] = split(block.T)
 
-    for chunk in range(CHUNKS):
-        pack(chunk)
-        send_chunk(chunk)
+    pack(0)
+    send_batch(0)
+    pack(1)
+    send_batch(1)
+    batch_left(0)
+    send_batch(2)
+    batch_left(1)
+    send_batch(3)
+    batch_left(2)
+    send_batch(4)
+    batch_left(3)
+    send_batch(5)
+    batch_left(4)
+    send_batch(6)
+    batch_left(5)
+    send_batch(7)
+    batch_left(6)
+    send_batch(8)
+    pack(2)
+    batch_left(7)
+    send_batch(9)
+    batch_left(8)
+    send_batch(10)
+    batch_left(9)
+    send_batch(11)
     take_chunk(0)
     multiply(0, 0)
+    batch_left(10)
+    send_batch(12)
+    batch_left(11)
+    send_batch(13)
+    batch_left(12)
+    send_batch(14)
+    batch_left(13)
+    send_batch(15)
+    batch_left(14)
+    send_batch(16)
+    pack(3)
+    batch_left(15)
+    send_batch(17)
+    batch_left(16)
+    send_batch(18)
     take_chunk(1)
     multiply(0, 1)
     to_core(0)
+    batch_left(17)
+    send_batch(19)
+    batch_left(18)
+    send_batch(20)
     to_xy(0)
+    batch_left(19)
+    send_batch(21)
+    batch_left(20)
+    send_batch(22)
     to_z(0)
+    batch_left(21)
+    send_batch(23)
+    batch_left(22)
+    send_batch(24)
     back_z(0)
-    back_xy(0)
+    batch_left(23)
+    send_batch(25)
     take_chunk(2)
     multiply(1, 2)
     to_core(1)
+    batch_left(24)
+    send_batch(26)
+    back_xy(0)
+    batch_left(25)
+    send_batch(27)
+    to_xy(1)
+    batch_left(26)
+    send_batch(28)
     back_core(0)
-    to_xy(1)
+    batch_left(27)
+    send_batch(29)
+    batch_left(28)
+    send_batch(30)
+    batch_left(29)
+    send_batch(31)
     finish(0)
-    to_z(1)
-    back_z(1)
-    back_xy(1)
     take_chunk(3)
     multiply(2, 3)
+    to_z(1)
     to_core(2)
     to_xy(2)
+    back_z(1)
+    to_z(2)
+    back_xy(1)
+    back_z(2)
     back_core(1)
     finish(1)
-    to_z(2)
-    back_z(2)
     back_xy(2)
     back_core(2)
     finish(2)
-
+    batch_left(30)
+    batch_left(31)
     for c in range(CHUNKS):
         basis_ref[pl.ds(256 * c, 256), :] = start[:, c].reshape(256, RANK)
 
@@ -330,24 +417,22 @@
         factor[:, c] = basis[256 * c : 256 * c + 256].reshape(NWA, 8, RANK)
     fh, fl = split(basis.T)
     both = jnp.concatenate([fh, fl], axis=0)
-    for q in range(8):
-        columns = pl.ds(128 * q, 128)
+    for q in range(4):
+        columns = pl.ds(256 * q, 256)
         wide = jnp.dot(both, high[:, columns], preferred_element_type=F32)
         cross = jnp.dot(fh, low[:, columns], preferred_element_type=F32)
-        tile = wide[:RANK] + (wide[RANK:] + cross)
-        for m in range(4):
-            core_out[4 * q + m] = tile[:, 32 * m : 32 * m + 32]
-
-    for chunk in range(CHUNKS):
-        others = packed.at[chunk, pl.ds(0, NWA - 1)]
-        pltpu.make_async_copy(others, others, send_sem.at[chunk]).wait()
+        tile = (wide[:RANK] + (wide[RANK:] + cross)).T
+        for m in range(8):
+            core_out[8 * q + m] = tile[32 * m : 32 * m + 32]
+
     for r in range(len(ROUNDS)):
-        wait(from_core.at[r], r, 0, 0)
-        wait(mine.at[r, pl.ds(0, NXY - 1)], r, 1, 0)
+        used = pl.ds(0, len(ROUNDS[r]))
+        wait(from_core.at[r, used], r, 0, 0)
+        wait(mine.at[r, pl.ds(0, NXY - 1), used], r, 1, 0)
         wait(sums.at[r, pl.ds(0, KZ - 1)], r, 2, 0)
         wait(gathered.at[r, pl.ds(0, KZ - 1)], r, 3, 0)
-        wait(mine.at[r, pl.ds(0, NXY - 1)], r, 4, 0)
-        wait(from_core.at[r], r, 5, 0)
+        wait(mine.at[r, pl.ds(0, NXY - 1), used], r, 4, 0)
+        wait(from_core.at[r, used], r, 5, 0)
 
 
 def per_device(tensor, start):
@@ -356,7 +441,7 @@
         kernel,
         out_shape=(
             jax.ShapeDtypeStruct((NWA, CHUNKS, 8, RANK), F32),
-            jax.ShapeDtypeStruct((PLANES, RANK, 32), F32),
+            jax.ShapeDtypeStruct((PLANES, 32, RANK), F32),
         ),
         in_specs=[pl.BlockSpec(memory_space=pl.ANY), pl.BlockSpec(memory_space=pltpu.VMEM)],
         out_specs=(pl.BlockSpec(memory_space=pltpu.VMEM),) * 2,
@@ -382,7 +467,7 @@
             pltpu.VMEM((NX, RANK), F32),
             pltpu.VMEM((RANK, RANK), F32),
             pltpu.SemaphoreType.DMA((CHUNKS,)),
-            pltpu.SemaphoreType.DMA((CHUNKS,)),
+            pltpu.SemaphoreType.DMA((CHUNKS, BATCHES)),
             pltpu.SemaphoreType.DMA((CHUNKS,)),
             pltpu.SemaphoreType.DMA((2, n, 6)),
         ],
@@ -391,7 +476,7 @@
         ),
         name="factor_core",
     )(tensor.reshape(PLANES, 32, NX), start.reshape(NWA, CHUNKS, 8, RANK))
-    return factor.reshape(NX, RANK), core.reshape(4, 8, RANK, 32)
+    return factor.reshape(NX, RANK), jnp.swapaxes(core.reshape(4, 8, 32, RANK), 2, 3)
 
 
 def solution(mesh):

time: 205 us -> 183 us (0.89)
  Pallas kernels: 199 us -> 178 us
    pallas_call x1, Pallas kernels: 199 us -> 178 us  [per_device(): pl.pallas_call(kernel, out_shape=(jax.ShapeDtypeStruct((NWA, CHUNKS, 8, R...]
where the time goes in v3:
time: 183 us
  Pallas kernels  178 us (97%)
  local copies, waits for them, and re-layouts  3.74 us (2%)
    pallas_call x1, Pallas kernels, per_device(): pl.pallas_call(kernel, out_shape=(jax.ShapeDtypeStruct((NWA, CHUNKS, 8, R...  178 us
    unnamed x2, local copies, waits for them, and re-layouts  3.74 us

profile of v3, /device:TPU:1, one launch (start us, length us, event | category | flops | bytes accessed | tf_op | source)
XLA Modules:
  0.0 182.7 jit_solution(13876228324332807278)
XLA Ops:
  0.6 178.4 %factor_core.1 = (f32[32,4,8,128]{3,2,1,0:T(8,128)}, f32[32,32,128]{2,1,0:T(8,128)}) custom-call(f32[32,32,1024]{2,1,0:T(8,128)} %bitcast.6, f32[32,4,8,128]{3,2,1,0:T(8,128)} %bitcast.7), custom_call_target="tpu_custom_call" | custom-call | tf_op jit(solution)/shard_map/factor_core/pallas_call | solution.py:440
  179.0 1.9 %copy.6 = f32[1024,128]{1,0:T(8,128)} copy(f32[1024,128]{1,0:T(8,128)} %bitcast.9) | data formatting | bytes 1048576
  180.9 1.9 %copy.7 = f32[4,8,128,32]{2,3,1,0:T(8,128)} copy(f32[4,8,128,32]{2,3,1,0:T(8,128)} %bitcast.8) | data formatting | bytes 1048576

commit v4 on v3

--- a/solution.py
+++ b/solution.py
@@ -53,9 +53,10 @@
             packed[chunk, 4 * group + m, :, pl.ds(pl.multiple_of(128 * quad, 128), 128)] = out[m]
 
 
-def inverse_factor(small, lower_inv):
+def inverse_factor(small, lower_inv, stage):
     lane = lax.broadcasted_iota(jnp.int32, (8, RANK), 1)
     full = (8, RANK)
+    sublane = lax.broadcasted_iota(jnp.int32, (8, RANK), 0)
     count = RANK // 8
     tiles = [small[8 * t : 8 * t + 8, :] for t in range(count)]
 
@@ -64,10 +65,14 @@
 
     def spread(t):
         cols = columns(t, t)
-        entry = {(i, s): jnp.broadcast_to(cols[s][i : i + 1, :], full) for s in range(8) for i in range(s, 8)}
+        slot = t % 2
+        for s in range(8):
+            stage[slot, s] = cols[s]
+        stage[slot, 8] = tiles[t]
+        entry = {(i, s): stage[slot, s, pl.ds(i, 8, stride=0), :] for s in range(8) for i in range(s, 8)}
         rows = []
         for s in range(8):
-            row = jnp.broadcast_to(tiles[t][s : s + 1, :], full)
+            row = stage[slot, 8, pl.ds(s, 8, stride=0), :]
             inside = (lane >= 8 * t) & (lane < 8 * t + 8)
             rows.append(jnp.where(inside, jnp.where(lane == 8 * t + s, 1.0, 0.0), row))
         return entry, rows
@@ -100,8 +105,20 @@
         if t + 1 < count:
             update(t + 1, t, lower, root, done)
             entry, rows = spread(t + 1)
-        for u in range(t + 2, count):
+        for u in range(t + 2, min(t + 3, count)):
             update(u, t, lower, root, done)
+        if t + 3 < count:
+            block = done[0]
+            for k in range(1, 8):
+                block = jnp.where(sublane == k, done[k], block)
+            hi, rest = block.astype(BF16), block - block.astype(BF16).astype(F32)
+            mid, lo = split(rest)
+            lhs = jnp.concatenate([hi, hi, hi, mid, mid, lo], axis=0)
+            rhs = jnp.concatenate([hi, mid, lo, hi, mid, hi], axis=0)
+            change = lax.dot_general(lhs, rhs, (((0,), (0,)), ((), ())), preferred_element_type=F32)
+            inside = (lane >= 8 * t) & (lane < 8 * t + 8)
+            for u in range(t + 3, count):
+                tiles[u] = jnp.where(inside, 0.0, tiles[u]) - change[8 * u : 8 * u + 8]
         for k in range(8):
             j = 8 * t + k
             lower_inv[j : j + 1, :] = jnp.where(lane <= j, done[k], 0.0)[0:1, :]
@@ -111,7 +128,7 @@
     tensor, start, factor, core_out,
     loaded, packed, landed, high, low,
     gram, from_core, mine, from_xy, sums, from_z, final, gathered, part, whole,
-    gram_high, gram_low, basis_ref, image_ref, lower_inv,
+    gram_high, gram_low, started, basis_ref, lower_inv, stage, factor_buf, core_buf,
     load_sem, send_sem, recv_sem, sem,
 ):
     me, gz = lax.axis_index("wa"), lax.axis_index("gz")
@@ -137,8 +154,12 @@
             tensor.at[:, pl.ds(8 * chunk, 8), :], loaded.at[chunk], load_sem.at[chunk]
         )
 
+    def load_start():
+        return pltpu.make_async_copy(start, started, load_sem.at[CHUNKS])
+
     for chunk in range(CHUNKS):
         load(chunk).start()
+    load_start().start()
     barrier = pltpu.get_barrier_semaphore()
 
     def greet(device):
@@ -153,7 +174,6 @@
         greet(xy_peer(step)[1])
 
     greet(sibling)
-    pl.semaphore_wait(barrier, NWA - 1 + NXY - 1 + 1)
 
     def pack(chunk):
         load(chunk).wait()
@@ -295,6 +315,7 @@
                 gram_high[rc, rb], gram_low[rc, rb] = split(block.T)
 
     pack(0)
+    pl.semaphore_wait(barrier, NWA - 1 + NXY - 1 + 1)
     send_batch(0)
     pack(1)
     send_batch(1)
@@ -348,38 +369,38 @@
     send_batch(21)
     batch_left(20)
     send_batch(22)
-    to_z(0)
     batch_left(21)
     send_batch(23)
+    to_z(0)
     batch_left(22)
     send_batch(24)
-    back_z(0)
     batch_left(23)
     send_batch(25)
+    batch_left(24)
+    send_batch(26)
     take_chunk(2)
     multiply(1, 2)
     to_core(1)
-    batch_left(24)
-    send_batch(26)
-    back_xy(0)
+    back_z(0)
     batch_left(25)
     send_batch(27)
-    to_xy(1)
     batch_left(26)
     send_batch(28)
-    back_core(0)
+    to_xy(1)
+    back_xy(0)
     batch_left(27)
     send_batch(29)
     batch_left(28)
     send_batch(30)
     batch_left(29)
     send_batch(31)
-    finish(0)
+    back_core(0)
     take_chunk(3)
     multiply(2, 3)
+    to_core(2)
     to_z(1)
-    to_core(2)
     to_xy(2)
+    finish(0)
     back_z(1)
     to_z(2)
     back_xy(1)
@@ -391,31 +412,31 @@
     finish(2)
     batch_left(30)
     batch_left(31)
+    load_start().wait()
     for c in range(CHUNKS):
-        basis_ref[pl.ds(256 * c, 256), :] = start[:, c].reshape(256, RANK)
+        basis_ref[:, pl.ds(256 * c, 256)] = started[:, c].reshape(256, RANK).T
 
     @pl.loop(0, ITERS)
     def _(step):
         bh, bl = split(basis_ref[...])
-        both = jnp.concatenate([bh, bl], axis=1)
-        for c in range(CHUNKS):
-            rows = pl.ds(256 * c, 256)
-            wide = jnp.dot(gram_high[rows, :], both, preferred_element_type=F32)
-            cross = jnp.dot(gram_low[rows, :], bh, preferred_element_type=F32)
-            image_ref[rows, :] = wide[:, :RANK] + (wide[:, RANK:] + cross)
-        image = image_ref[...]
+        both = jnp.concatenate([bh, bl], axis=0)
+        wide = jnp.dot(both, gram_high[...], preferred_element_type=F32)
+        cross = jnp.dot(bh, gram_low[...], preferred_element_type=F32)
+        image = wide[:RANK] + (wide[RANK:] + cross)
         small = lax.dot_general(
-            image, image, (((0,), (0,)), ((), ())), precision=lax.Precision.HIGHEST, preferred_element_type=F32
+            image, image, NT, precision=lax.Precision.HIGHEST, preferred_element_type=F32
         )
-        inverse_factor(small, lower_inv)
-        basis_ref[...] = lax.dot_general(
-            image, lower_inv[...], NT, precision=lax.Precision.HIGHEST, preferred_element_type=F32
+        inverse_factor(small, lower_inv, stage)
+        basis_ref[...] = jnp.dot(
+            lower_inv[...], image, precision=lax.Precision.HIGHEST, preferred_element_type=F32
         )
 
     basis = basis_ref[...]
     for c in range(CHUNKS):
-        factor[:, c] = basis[256 * c : 256 * c + 256].reshape(NWA, 8, RANK)
-    fh, fl = split(basis.T)
+        factor_buf[:, c] = basis[:, 256 * c : 256 * c + 256].T.reshape(NWA, 8, RANK)
+    stored = [pltpu.make_async_copy(factor_buf, factor, load_sem.at[0])]
+    stored[0].start()
+    fh, fl = split(basis)
     both = jnp.concatenate([fh, fl], axis=0)
     for q in range(4):
         columns = pl.ds(256 * q, 256)
@@ -423,7 +444,10 @@
         cross = jnp.dot(fh, low[:, columns], preferred_element_type=F32)
         tile = (wide[:RANK] + (wide[RANK:] + cross)).T
         for m in range(8):
-            core_out[8 * q + m] = tile[32 * m : 32 * m + 32]
+            core_buf[8 * q + m] = tile[32 * m : 32 * m + 32]
+        planes = pl.ds(8 * q, 8)
+        stored.append(pltpu.make_async_copy(core_buf.at[planes], core_out.at[planes], load_sem.at[1 + q]))
+        stored[-1].start()
 
     for r in range(len(ROUNDS)):
         used = pl.ds(0, len(ROUNDS[r]))
@@ -433,6 +457,8 @@
         wait(gathered.at[r, pl.ds(0, KZ - 1)], r, 3, 0)
         wait(mine.at[r, pl.ds(0, NXY - 1), used], r, 4, 0)
         wait(from_core.at[r, used], r, 5, 0)
+    for copy in stored:
+        copy.wait()
 
 
 def per_device(tensor, start):
@@ -443,8 +469,8 @@
             jax.ShapeDtypeStruct((NWA, CHUNKS, 8, RANK), F32),
             jax.ShapeDtypeStruct((PLANES, 32, RANK), F32),
         ),
-        in_specs=[pl.BlockSpec(memory_space=pl.ANY), pl.BlockSpec(memory_space=pltpu.VMEM)],
-        out_specs=(pl.BlockSpec(memory_space=pltpu.VMEM),) * 2,
+        in_specs=[pl.BlockSpec(memory_space=pl.ANY)] * 2,
+        out_specs=(pl.BlockSpec(memory_space=pl.ANY),) * 2,
         scratch_shapes=[
             pltpu.VMEM((CHUNKS, PLANES, 8, NX), F32),
             pltpu.VMEM((CHUNKS, NWA, 8, NX), F32),
@@ -463,10 +489,13 @@
             pltpu.VMEM((n, SLOTS, 2, 256, 128), F32),
             pltpu.VMEM((NX, NX), BF16),
             pltpu.VMEM((NX, NX), BF16),
-            pltpu.VMEM((NX, RANK), F32),
-            pltpu.VMEM((NX, RANK), F32),
+            pltpu.VMEM((NWA, CHUNKS, 8, RANK), F32),
+            pltpu.VMEM((RANK, NX), F32),
             pltpu.VMEM((RANK, RANK), F32),
-            pltpu.SemaphoreType.DMA((CHUNKS,)),
+            pltpu.VMEM((2, 9, 8, RANK), F32),
+            pltpu.VMEM((NWA, CHUNKS, 8, RANK), F32),
+            pltpu.VMEM((PLANES, 32, RANK), F32),
+            pltpu.SemaphoreType.DMA((CHUNKS + 1,)),
             pltpu.SemaphoreType.DMA((CHUNKS, BATCHES)),
             pltpu.SemaphoreType.DMA((CHUNKS,)),
             pltpu.SemaphoreType.DMA((2, n, 6)),

time: 183 us -> 174 us (0.951)
  Pallas kernels: 178 us -> 169 us
    pallas_call x1, Pallas kernels: 178 us -> 169 us  [per_device(): pl.pallas_call(kernel, out_shape=(jax.ShapeDtypeStruct((NWA, CHUNKS, 8, R...]
where the time goes in v4:
time: 174 us
  Pallas kernels  169 us (97%)
  local copies, waits for them, and re-layouts  3.74 us (2%)
    pallas_call x1, Pallas kernels, per_device(): pl.pallas_call(kernel, out_shape=(jax.ShapeDtypeStruct((NWA, CHUNKS, 8, R...  169 us
    unnamed x2, local copies, waits for them, and re-layouts  3.74 us

profile of v4, /device:TPU:1, one launch (start us, length us, event | category | flops | bytes accessed | tf_op | source)
XLA Modules:
  0.0 173.5 jit_solution(10924052158622935315)
XLA Ops:
  0.6 169.2 %factor_core.1 = (f32[32,4,8,128]{3,2,1,0:T(8,128)}, f32[32,32,128]{2,1,0:T(8,128)}) custom-call(f32[32,32,1024]{2,1,0:T(8,128)} %bitcast.6, f32[32,4,8,128]{3,2,1,0:T(8,128)} %bitcast.7), custom_call_target="tpu_custom_call" | custom-call | tf_op jit(solution)/shard_map/factor_core/pallas_call | solution.py:466
  169.8 1.9 %copy.6 = f32[1024,128]{1,0:T(8,128)} copy(f32[1024,128]{1,0:T(8,128)} %bitcast.9) | data formatting | bytes 1048576
  171.7 1.9 %copy.7 = f32[4,8,128,32]{2,3,1,0:T(8,128)} copy(f32[4,8,128,32]{2,3,1,0:T(8,128)} %bitcast.8) | data formatting | bytes 1048576

commit v5 on v4

--- a/solution.py
+++ b/solution.py
@@ -23,6 +23,10 @@
     [(0, 3), (1, 3), (2, 3), (3, 3)],
 ]
 SLOTS = 4
+OFFSETS = [
+    (2, 2), (2, 1), (1, 2), (2, 3), (3, 2), (2, 0), (0, 2), (1, 1),
+    (3, 3), (1, 3), (3, 1), (1, 0), (0, 1), (3, 0), (0, 3),
+]
 NXY = KX * KY
 TILES = SLOTS * 2
 F32, BF16 = jnp.float32, jnp.bfloat16
@@ -141,9 +145,9 @@
     def peer(step):
         return lax.rem(me + step, NWA)
 
-    def xy_peer(step):
-        q = lax.rem(me_xy + step, NXY)
-        return q, {"wa": (q // KY) * KZ + z, "gz": lax.rem(q, KY) * 2 + core}
+    def xy_peer(offset):
+        to_x, to_y = lax.rem(x + offset[0], KX), lax.rem(y + offset[1], KY)
+        return to_x * KY + to_y, {"wa": to_x * KZ + z, "gz": to_y * 2 + core}
 
     def z_peer(step):
         q = lax.rem(z + step, KZ)
@@ -169,9 +173,8 @@
     def _(step):
         greet({"wa": peer(step)})
 
-    @pl.loop(1, NXY)
-    def _(step):
-        greet(xy_peer(step)[1])
+    for offset in OFFSETS:
+        greet(xy_peer(offset)[1])
 
     greet(sibling)
 
@@ -192,8 +195,9 @@
 
         @pl.loop(first, end)
         def _(step):
-            half = lax.div(step + 1, 2)
-            to = peer(jnp.where(lax.rem(step, 2) == 1, half, NWA - half))
+            rank = NWA - step
+            half = lax.div(rank + 1, 2)
+            to = peer(jnp.where(lax.rem(rank, 2) == 1, half, NWA - half))
             pltpu.make_async_remote_copy(
                 src_ref=packed.at[chunk, to],
                 dst_ref=landed.at[chunk, me],
@@ -249,9 +253,8 @@
         for slot in range(len(ROUNDS[r])):
             mine[r, :, slot] = (gram[r, slot, core] + from_core[r, slot]).reshape(NXY, 16, 128)
 
-        @pl.loop(1, NXY)
-        def _(step):
-            q, device = xy_peer(step)
+        for offset in OFFSETS:
+            q, device = xy_peer(offset)
             send(mine.at[r, q, used], from_xy.at[r, me_xy, used], r, 1, device)
 
         from_xy[r, me_xy, used] = mine[r, me_xy, used]
@@ -293,9 +296,8 @@
         used = pl.ds(0, n)
         part[r, used] = gathered[r, pl.ds(0, 2 * n)].reshape(n, 16, 128)
 
-        @pl.loop(1, NXY)
-        def _(step):
-            q, device = xy_peer(step)
+        for offset in OFFSETS:
+            q, device = xy_peer(offset)
             send(part.at[r, used], whole.at[r, used, core, share, :], r, 4, device)
 
         whole[r, used, core, share, :] = part[r, used]
@@ -427,9 +429,11 @@
             image, image, NT, precision=lax.Precision.HIGHEST, preferred_element_type=F32
         )
         inverse_factor(small, lower_inv, stage)
-        basis_ref[...] = jnp.dot(
-            lower_inv[...], image, precision=lax.Precision.HIGHEST, preferred_element_type=F32
-        )
+        ih, il = split(image)
+        lh, ll = split(lower_inv[...])
+        wide = jnp.dot(jnp.concatenate([lh, ll], axis=0), ih, preferred_element_type=F32)
+        cross = jnp.dot(lh, il, preferred_element_type=F32)
+        basis_ref[...] = wide[:RANK] + (wide[RANK:] + cross)
 
     basis = basis_ref[...]
     for c in range(CHUNKS):
@@ -459,6 +463,39 @@
         wait(from_core.at[r, used], r, 5, 0)
     for copy in stored:
         copy.wait()
+
+
+def hand_over_kernel(factor, core, factor_out, core_out, buffers, sem):
+    pairs = [(factor, factor_out), (core, core_out)]
+    pieces = [(k, pl.ds(16 * part, 16)) for part in range(2) for k in range(2)]
+
+    def fetch(n):
+        k, rows = pieces[n]
+        return pltpu.make_async_copy(pairs[k][0].at[rows], buffers.at[k, rows], sem.at[0, n])
+
+    def store(n):
+        k, rows = pieces[n]
+        return pltpu.make_async_copy(buffers.at[k, rows], pairs[k][1].at[rows], sem.at[1, n])
+
+    for n in range(len(pieces)):
+        fetch(n).start()
+    for n in range(len(pieces)):
+        fetch(n).wait()
+        store(n).start()
+    for n in range(len(pieces)):
+        store(n).wait()
+
+
+def hand_over(factor, core):
+    shape = jax.ShapeDtypeStruct((32, 32, RANK), F32)
+    return pl.pallas_call(
+        hand_over_kernel,
+        out_shape=(shape, shape),
+        in_specs=[pl.BlockSpec(memory_space=pl.ANY)] * 2,
+        out_specs=(pl.BlockSpec(memory_space=pl.ANY),) * 2,
+        scratch_shapes=[pltpu.VMEM((2, 32, 32, RANK), F32), pltpu.SemaphoreType.DMA((2, 4))],
+        name="hand_over",
+    )(factor, core)
 
 
 def per_device(tensor, start):
@@ -505,6 +542,7 @@
         ),
         name="factor_core",
     )(tensor.reshape(PLANES, 32, NX), start.reshape(NWA, CHUNKS, 8, RANK))
+    factor, core = hand_over(factor.reshape(32, 32, RANK), core)
     return factor.reshape(NX, RANK), jnp.swapaxes(core.reshape(4, 8, 32, RANK), 2, 3)
 
 

time: 174 us -> 163 us (0.937)
  Pallas kernels: 169 us -> 163 us
  local copies, waits for them, and re-layouts: 3.74 us -> 0 us
    pallas_call x1, Pallas kernels: 169 us -> 161 us  [per_device(): pl.pallas_call(kernel, out_shape=(jax.ShapeDtypeStruct((NWA, CHUNKS, 8, R...]
    unnamed x2 -> x0, local copies, waits for them, and re-layouts: 3.74 us -> none
    pallas_call x0 -> x1, Pallas kernels: none -> 1.98 us  [hand_over(): pl.pallas_call(hand_over_kernel, out_shape=(shape, shape), in_specs=[pl.B...]
where the time goes in v5:
time: 163 us
  Pallas kernels  163 us (100%)
    pallas_call x1, Pallas kernels, per_device(): pl.pallas_call(kernel, out_shape=(jax.ShapeDtypeStruct((NWA, CHUNKS, 8, R...  161 us

profile of v5, /device:TPU:1, one launch (start us, length us, event | category | flops | bytes accessed | tf_op | source)
XLA Modules:
  0.0 163.4 jit_solution(15304946926585615546)
XLA Ops:
  0.6 160.8 %factor_core.1 = (f32[32,4,8,128]{3,2,1,0:T(8,128)}, f32[32,32,128]{2,1,0:T(8,128)}) custom-call(f32[32,32,1024]{2,1,0:T(8,128)} %bitcast.7, f32[32,4,8,128]{3,2,1,0:T(8,128)} %bitcast.8), custom_call_target="tpu_custom_call" | custom-call | tf_op jit(solution)/shard_map/factor_core/pallas_call | solution.py:503
  161.4 2.0 %hand_over.1 = (f32[32,32,128]{2,1,0:T(8,128)}, f32[32,32,128]{2,1,0:T(8,128)}) custom-call(f32[32,32,128]{2,1,0:T(8,128)} %bitcast.9, f32[32,32,128]{2,1,0:T(8,128)} %get-tuple-element.7.core), custom_call_target="tpu_custom_call" | custom-call | tf_op jit(solution)/shard_map/hand_over/pallas_call | solution.py:491

commit v6 on v5

--- a/solution.py
+++ b/solution.py
@@ -397,10 +397,10 @@
     batch_left(29)
     send_batch(31)
     back_core(0)
+    to_z(1)
     take_chunk(3)
     multiply(2, 3)
     to_core(2)
-    to_z(1)
     to_xy(2)
     finish(0)
     back_z(1)

time: 163 us -> 163 us (level)
  no operation moved by 1% of the time
where the time goes in v6:
time: 163 us
  Pallas kernels  162 us (99%)
    pallas_call x1, Pallas kernels, per_device(): pl.pallas_call(kernel, out_shape=(jax.ShapeDtypeStruct((NWA, CHUNKS, 8, R...  160 us

profile of v6, /device:TPU:1, one launch (start us, length us, event | category | flops | bytes accessed | tf_op | source)
XLA Modules:
  0.0 163.1 jit_solution(14500759136268491962)
XLA Ops:
  0.6 160.4 %factor_core.1 = (f32[32,4,8,128]{3,2,1,0:T(8,128)}, f32[32,32,128]{2,1,0:T(8,128)}) custom-call(f32[32,32,1024]{2,1,0:T(8,128)} %bitcast.7, f32[32,4,8,128]{3,2,1,0:T(8,128)} %bitcast.8), custom_call_target="tpu_custom_call" | custom-call | tf_op jit(solution)/shard_map/factor_core/pallas_call | solution.py:503
  161.1 2.0 %hand_over.1 = (f32[32,32,128]{2,1,0:T(8,128)}, f32[32,32,128]{2,1,0:T(8,128)}) custom-call(f32[32,32,128]{2,1,0:T(8,128)} %bitcast.9, f32[32,32,128]{2,1,0:T(8,128)} %get-tuple-element.7.core), custom_call_target="tpu_custom_call" | custom-call | tf_op jit(solution)/shard_map/hand_over/pallas_call | solution.py:491
